TPU v7x, 32 devices: a whole 2x2x4 slice. The times are simulated.
32 devices in a mesh: row: 8 (over y, x, core), col: 4 (over z).
Axes of the slice: x: 2, y: 2, z: 4, core: 2. Of those that a mesh axis runs over, the one named last changes fastest.
Arguments:
- values: float32 [4096, 4096], P('row', 'col'), may hold values from 0 to 10, as said below
- pattern: int32 [32, 32], replicated, may hold values from 0 to 1, as said below
- pruning: int32 [32, 32], replicated, may hold values from 0 to 1, as said below
- owners: int32 [32], replicated, may hold values from 0 to 31, as said below
Outputs:
- expanded: float32 [4096, 4096], P('row', 'col')
Inputs may be any that keep to these rules, and one draw needn't show every extreme that they name: `values`: positive scores. `pattern`: every diagonal block is present. `pruning`: every diagonal block is kept. `owners`: A permutation of the 32 column blocks. Of the 8 column blocks of one index of col, at most 2 are stored at the column blocks of any one index of col, and exactly 2 at those of some index.
All inputs are finite; a program needn't handle non-finite values.
Results may differ from a plain program's by a relative error of at most 0.00065.
Values may be sent and summed in bfloat16 or wider, within the bound.
A program may use at most 128 MiB of HBM per device.

v0:
```python
import jax
import jax.numpy as jnp
from jax import lax
from jax.sharding import PartitionSpec as P

BLK = 128


def expand_mask(tile, mask, blk):
    rows_in, cols_in = tile.shape
    shaped = tile.reshape(rows_in // blk, blk, cols_in // blk, blk)
    return (shaped * mask.astype(tile.dtype)[:, None, :, None]).reshape(rows_in, cols_in)


def ranks_of(destination):
    width = destination.shape[-1]
    earlier = jnp.arange(width)[:, None] < jnp.arange(width)[None, :]
    same_dest = destination[..., :, None] == destination[..., None, :]
    return jnp.sum(jnp.where(same_dest & earlier, 1, 0), axis=-2).astype(jnp.int32)


def pack_blocks(tile, owners, me_col, ncols, capacity, blk):
    rows_in, cols_in = tile.shape
    width = cols_in // blk
    my_owners = lax.dynamic_slice(owners, (me_col * width,), (width,))
    destination = my_owners // width
    rank = ranks_of(destination)
    slot_ids = jnp.arange(ncols * capacity)
    selector = (
        (destination[None, :] == (slot_ids // capacity)[:, None])
        & (rank[None, :] == (slot_ids % capacity)[:, None])
    ).astype(tile.dtype)
    column_blocks = tile.reshape(rows_in, width, blk)
    outgoing = jnp.einsum(
        "pk,rkb->prb",
        selector,
        column_blocks,
        preferred_element_type=jnp.float32,
        precision=lax.Precision.HIGHEST,
    )
    return outgoing.astype(tile.dtype)


def unpack_blocks(arrived, owners, me_col, ncols, capacity):
    slot_count, rows_in, blk = arrived.shape
    width = owners.shape[0] // ncols
    table = owners.reshape(ncols, width)
    rank = ranks_of(table // width)
    wanted = me_col * width + jnp.arange(width)
    matches = table[None, :, :] == wanted[:, None, None]
    which_slot = rank[:, :, None] == jnp.arange(capacity)[None, None, :]
    selector = jnp.sum(jnp.where(matches[:, :, :, None] & which_slot[None], 1, 0), axis=2)
    selector = selector.reshape(width, ncols * capacity).astype(arrived.dtype)
    placed = jnp.einsum(
        "sp,prb->rsb",
        selector,
        arrived,
        preferred_element_type=jnp.float32,
        precision=lax.Precision.HIGHEST,
    )
    return placed.reshape(rows_in, width * blk).astype(arrived.dtype)


def body(values, pattern, pruning, owners):
    rows_dev, cols_dev = values.shape
    blk = BLK
    row_blocks = rows_dev // blk
    col_blocks = cols_dev // blk
    ncols = lax.axis_size("col")
    capacity = max(2, (col_blocks + ncols - 1) // ncols)
    me_row = lax.axis_index("row")
    me_col = lax.axis_index("col")
    local_pattern = lax.dynamic_slice(
        pattern, (me_row * row_blocks, me_col * col_blocks), (row_blocks, col_blocks)
    )
    masked = expand_mask(values, local_pattern, blk)
    colsum_in = lax.psum(jnp.sum(masked, axis=0), "row")
    stochastic = (masked / colsum_in[None, :]).astype(jnp.bfloat16)
    row_panel = lax.all_gather(stochastic, "col", axis=1, tiled=True)
    nodes = row_panel.shape[1]
    pruning_rows = lax.dynamic_slice(
        pruning, (me_row * row_blocks, 0), (row_blocks, pruning.shape[1])
    )
    arrived = lax.all_to_all(
        pack_blocks(stochastic, owners, me_col, ncols, capacity, blk),
        "col",
        split_axis=0,
        concat_axis=0,
        tiled=True,
    )
    right_operand = unpack_blocks(arrived, owners, me_col, ncols, capacity)
    wanted = me_col * col_blocks + jnp.arange(col_blocks)
    relocate = (owners[:, None] == wanted[None, :]).astype(jnp.float32)
    kept_mask = jnp.dot(pruning_rows.astype(jnp.float32), relocate, precision=lax.Precision.HIGHEST)
    square = jnp.dot(
        row_panel,
        lax.all_gather(right_operand, "row", axis=0, tiled=True),
        preferred_element_type=jnp.float32,
    )
    inflated = expand_mask(square * square, kept_mask, blk)
    colsum_out = lax.psum(jnp.sum(inflated, axis=0), "row")
    normalized = jnp.float32(nodes) * inflated / colsum_out[None, :]
    return normalized


def solution(mesh):
    return jax.shard_map(
        body,
        mesh=mesh,
        in_specs=(P("row", "col"), P(), P(), P()),
        out_specs=P("row", "col"),
        check_vma=False,
    )
```

profile of v0, /device:TPU:0, one launch (start us, length us, event | category | flops | bytes accessed | tf_op | source)
XLA Modules:
  0.0 212.4 jit_solution(5974674823974820582)
XLA Ops:
  6.5 0.0 all-gather.3.cloned.1.call-start
  6.5 0.0 copy-start
  6.5 0.9 dynamic-slice_convert_fusion
  7.4 0.2 mul.43
  7.7 0.5 copy-done
  8.1 0.7 fusion.1
  8.8 15.1 %psum.14 = f32[1024]{0:T(1024)S(1)} all-reduce(f32[1024]{0:T(1024)S(1)} %fusion.1), channel_id=1, replica_groups=mesh['row'=8,'col'=4] {'row'}, use_global_device_ids=true, to_apply=%region_1.0 | all-reduce | flops 1024 | bytes 8192 | tf_op jit(solution)/shard_map/psum | solution.py:77
  24.0 3.2 %divide_convert_fusion = bf16[512,1024]{1,0:T(8,128)(2,1)} fusion(f32[1024]{0:T(1024)S(1)} %psum.14, f32[512,1024]{1,0:T(8,128)} %param.4, f32[64,8,8,128]{3,2,1,0:T(8,128)S(1)} %bitcast.30), kind=kLoop, calls=%fused_computation.3 | loop fusion | flops 1572864 | bytes 5246976 | tf_op jit(solution)/shard_map/convert_element_type | solution.py:78
  27.2 0.0 all-gather.3.cloned.1.call-update
  27.2 1.5 copy.14
  28.7 0.0 copy-done.1
  28.7 0.1 and_select_fusion.2
  28.8 0.1 select_reduce_fusion.2
  28.9 0.5 convolution_convert_fusion
  29.4 1.2 copy.8
  30.6 4.9 %all-to-all-start = ((bf16[8,512,128]{2,1,0:T(8,128)(2,1)}), bf16[8,512,128]{2,1,0:T(8,128)(2,1)S(1)}, u32[]{:S(2)}, u32[]{:S(2)}) async-start(bf16[8,512,128]{2,1,0:T(8,128)(2,1)} %copy.8), calls=%async_computation | async-start | bytes 2097152 | tf_op jit(solution)/shard_map/all_to_all | solution.py:84
  35.4 0.0 all-gather.5.cloned.1.call-start
  35.4 0.1 eq.109
  35.5 0.1 select_reduce_fusion.1
  35.6 0.1 broadcast_compare_fusion
  35.7 0.2 select_reduce_fusion
  35.9 51.6 %all-to-all-done = bf16[8,512,128]{2,1,0:T(8,128)(2,1)S(1)} async-done(((bf16[8,512,128]{2,1,0:T(8,128)(2,1)}), bf16[8,512,128]{2,1,0:T(8,128)(2,1)S(1)}, u32[]{:S(2)}, u32[]{:S(2)}) %all-to-all-start) | async-done | bytes 1048608 | tf_op jit(solution)/shard_map/all_to_all | solution.py:84
  87.6 0.7 convolution_convert_fusion.1
  88.3 1.3 copy.26
  89.6 0.0 all-gather.5.cloned.1.call-update
  89.7 0.9 fusion.2
  90.5 36.8 %all-gather.3.cloned.1.call-done = bf16[512,4096]{1,0:T(8,128)(2,1)} async-done(((bf16[512,1024]{1,0:T(8,128)(2,1)}), bf16[512,4096]{1,0:T(8,128)(2,1)}) %all-gather.3.cloned.1.call-update) | async-done | bytes 4194320 | tf_op jit(solution)/shard_map/all_gather | solution.py:79
  127.3 54.9 %all-gather.5.cloned.1.call-done = bf16[4096,1024]{1,0:T(8,128)(2,1)} async-done(((bf16[512,1024]{1,0:T(8,128)(2,1)}), bf16[4096,1024]{1,0:T(8,128)(2,1)}) %all-gather.5.cloned.1.call-update) | async-done | bytes 8388624 | tf_op jit(solution)/shard_map/all_gather | solution.py:97
  182.2 0.2 mul.47
  182.4 8.4 %fusion.19 = (f32[1024]{0:T(1024)S(1)}, f32[512,1024]{1,0:T(8,128)S(1)}) fusion(f32[64,8,8,128]{3,2,1,0:T(8,128)S(1)} %bitcast.35, bf16[512,4096]{1,0:T(8,128)(2,1)} %all-gather.3.cloned.1.call-done, bf16[4096,1024]{1,0:T(8,128)(2,1)} %all-gather.5.cloned.1.call-done), kind=kOutput, calls=%fused_computation.48 | convolution fusion | flops 4296539136 | bytes 16781312 | tf_op jit(solution)/shard_map/dot_general | solution.py:95
  190.9 13.1 %psum.15 = f32[1024]{0:T(1024)S(1)} all-reduce(f32[1024]{0:T(1024)S(1)} %get-tuple-element.5), channel_id=1, replica_groups=mesh['row'=8,'col'=4] {'row'}, use_global_device_ids=true, to_apply=%region_6.7 | all-reduce | flops 1024 | bytes 8192 | tf_op jit(solution)/shard_map/psum | solution.py:101
  204.0 1.6 multiply_divide_fusion
  (7 shorter events, 0.0 us)
Async XLA Ops:
  6.5 120.8 %all-gather.3.cloned.1.call-start = ((), (), s32[]{:S(2)}) async-start(), calls=%async_computation.1 | async-start | bytes 5242880 | tf_op jit(solution)/shard_map/all_gather | solution.py:79
  6.5 1.6 copy-start
  27.2 1.5 copy-start.1
  30.6 57.0 %all-to-all-start = ((bf16[8,512,128]{2,1,0:T(8,128)(2,1)}), bf16[8,512,128]{2,1,0:T(8,128)(2,1)S(1)}, u32[]{:S(2)}, u32[]{:S(2)}) async-start(bf16[8,512,128]{2,1,0:T(8,128)(2,1)} %copy.8), calls=%async_computation | async-start | bytes 2097152 | tf_op jit(solution)/shard_map/all_to_all | solution.py:84
  35.4 146.8 %all-gather.5.cloned.1.call-start = ((), (), s32[]{:S(2)}) async-start(), calls=%async_computation.2 | async-start | bytes 9437184 | tf_op jit(solution)/shard_map/all_gather | solution.py:97
Sparse Core Ops, SparseCore 0:
  27.3 99.9 all-gather.2
  129.2 52.9 all-gather.4
where the time goes:
time: 213 us; the launch traced here: 212 us
  waiting for transfers between devices  143 us (67%)
  blocking collectives  28.2 us (13%)
  between operations  13.5 us (6%)
  matrix products  10.5 us (5%)
  other arithmetic  7.02 us (3%)
  local copies, waits for them, and re-layouts  4.96 us (2%)
  starting transfers between devices  4.87 us (2%)
    all_gather x1, waiting for transfers between devices, body(): lax.all_gather(right_operand, 'row', axis=0, tiled=True)  54.9 us
    all_to_all x1, waiting for transfers between devices, body(): lax.all_to_all(pack_blocks(stochastic, owners, me_col, ncols, capacity, b...  51.6 us
    all_gather x1, waiting for transfers between devices, body(): row_panel = lax.all_gather(stochastic, 'col', axis=1, tiled=True)  36.8 us
    psum x1, blocking collectives, body(): colsum_in = lax.psum(jnp.sum(masked, axis=0), 'row')  15.1 us
    psum x1, blocking collectives, body(): colsum_out = lax.psum(jnp.sum(inflated, axis=0), 'row')  13.1 us
    dot_general x1, matrix products, body(): jnp.dot(row_panel, lax.all_gather(right_operand, 'row', axis=0, tiled=Tru...  8.44 us
    all_to_all x1, starting transfers between devices, body(): lax.all_to_all(pack_blocks(stochastic, owners, me_col, ncols, capacity, b...  4.87 us
  transfers between devices with their start and end apart: 3, of which 3 were waited for; matrix products, arithmetic and copies ran while one was open for 3% of the time, Pallas kernels for 0%

commit v1 on v0

--- a/solution.py
+++ b/solution.py
@@ -1,6 +1,10 @@
+import functools
+
 import jax
 import jax.numpy as jnp
 from jax import lax
+from jax.experimental import pallas as pl
+from jax.experimental.pallas import tpu as pltpu
 from jax.sharding import PartitionSpec as P
 
 BLK = 128
@@ -103,9 +107,332 @@
     return normalized
 
 
+MESH = pl.DeviceIdType.MESH
+
+
+def tables(pattern, pruning, owners, rows_b, cols_b, ncols):
+    me_row = lax.axis_index("row")
+    me_col = lax.axis_index("col")
+    nblk = owners.shape[0]
+    ids = jnp.arange(nblk)
+    source = ids // cols_b
+    dest = owners // cols_b
+    same = (source[:, None] == source[None, :]) & (dest[:, None] == dest[None, :])
+    rank = jnp.sum(jnp.where(same & (ids[:, None] < ids[None, :]), 1, 0), axis=0)
+    cap = cols_b // ncols
+    packed = source * cols_b + dest * cap + rank
+    order = jnp.sum(jnp.where(packed[None, :] == ids[:, None], ids[None, :], 0), axis=1)
+    wanted = me_col * cols_b + jnp.arange(cols_b)
+    hit = owners[None, :] == wanted[:, None]
+    pos = jnp.sum(jnp.where(hit, (source * cap + rank)[None, :], 0), axis=1)
+    from_block = jnp.sum(jnp.where(hit, ids[None, :], 0), axis=1)
+    mine = lax.dynamic_slice(order, (me_col * cols_b,), (cols_b,))
+    prow = lax.dynamic_slice(pattern, (me_row * rows_b, 0), (rows_b, nblk))
+    prow = jnp.sum(jnp.where(mine[None, :, None] == ids[None, None, :], prow[:, None, :], 0), axis=2)
+    krow = lax.dynamic_slice(pruning, (me_row * rows_b, 0), (rows_b, nblk))
+    kept = jnp.sum(jnp.where(from_block[None, :, None] == ids[None, None, :], krow[:, None, :], 0), axis=2)
+    return jnp.concatenate(
+        [order, pos, prow.reshape(-1), kept.reshape(-1), mine - me_col * cols_b]
+    ).astype(jnp.int32)
+
+
+def kernel(n, nodes, tab, values, out, tiles, right, scores, work, sums_a, sums_b, rhs,
+           load_sem, zs, zr, xs, xr, as_, ar, bs, br):
+    rows, cols = values.shape
+    blk = BLK
+    rows_b, cols_b = rows // blk, cols // blk
+    nblk = n * cols_b
+    wide = cols // n
+    each = cols_b // n
+    half = rows_b // 2
+    loads = [
+        pltpu.make_async_copy(values.at[:, pl.ds(b * blk, blk)], scores.at[b], load_sem.at[b])
+        for b in range(cols_b)
+    ]
+    for load in loads:
+        load.start()
+    r = lax.axis_index("row")
+    c = lax.axis_index("col")
+    core, px, py = r % 2, (r // 2) % 2, r // 4
+
+    def at(fy, fx, fc):
+        y = 1 - py if fy else py
+        x = 1 - px if fx else px
+        k = 1 - core if fc else core
+        return y * 4 + x * 2 + k
+
+    others = [at(f // 4, (f // 2) % 2, f % 2) for f in range(1, 8)]
+
+    barrier = pltpu.get_barrier_semaphore()
+    for peer in others:
+        pl.semaphore_signal(barrier, inc=1, device_id={"row": peer}, device_id_type=MESH)
+
+    @pl.when(c > 0)
+    def _():
+        pl.semaphore_signal(barrier, inc=1, device_id={"col": c - 1}, device_id_type=MESH)
+
+    @pl.when(c < n - 1)
+    def _():
+        pl.semaphore_signal(barrier, inc=1, device_id={"col": c + 1}, device_id_type=MESH)
+
+    def total_over_row(sums, ssem, rsem):
+        for f, peer in enumerate(others):
+            pltpu.make_async_remote_copy(
+                src_ref=sums.at[0], dst_ref=sums.at[f + 1], send_sem=ssem.at[f], recv_sem=rsem.at[f],
+                device_id={"row": peer}, device_id_type=MESH).start()
+        for f, peer in enumerate(others):
+            pltpu.make_async_remote_copy(
+                src_ref=sums.at[0], dst_ref=sums.at[f + 1], send_sem=ssem.at[f], recv_sem=rsem.at[f],
+                device_id={"row": peer}, device_id_type=MESH).wait()
+        terms = [sums[f] for f in range(8)]
+        pair = [terms[i] + terms[i + 1] for i in range(0, 8, 2)]
+        quad = [pair[0] + pair[1], pair[2] + pair[3]]
+        return quad[0] + quad[1]
+
+    for load in loads:
+        load.wait()
+    masks = nblk + cols_b
+    local = masks + 2 * rows_b * cols_b
+    for p in range(cols_b):
+        b = tab[local + p]
+        acc = jnp.zeros((1, blk), jnp.float32)
+        for i in range(rows_b):
+            keep = tab[masks + i * cols_b + p].astype(jnp.float32)
+            x = scores[b, pl.ds(i * blk, blk), :] * keep
+            work[p, pl.ds(i * blk, blk), :] = x
+            acc = acc + jnp.sum(x, axis=0, keepdims=True)
+        sums_a[0, :, pl.ds(p * blk, blk)] = acc
+
+    ends = jnp.where(c == 0, 1, 0) + jnp.where(c == n - 1, 1, 0)
+    pl.semaphore_wait(barrier, 9 - ends)
+
+    colsum = total_over_row(sums_a, as_, ar)
+    for p in range(cols_b):
+        part = work[p] / colsum[:, p * blk:(p + 1) * blk]
+        tiles[c, p // each, :, pl.ds(p % each * blk, blk)] = part.astype(jnp.bfloat16)
+
+    def zcopy(way, d, q, source):
+        target = c - 1 if way == 0 else c + 1
+        return pltpu.make_async_remote_copy(
+            src_ref=tiles.at[source, q], dst_ref=tiles.at[source, q],
+            send_sem=zs.at[way, d, q], recv_sem=zr.at[way, d, q],
+            device_id={"col": target}, device_id_type=MESH)
+
+    def zarrive(way, d, q, source):
+        peer = c + 1 if way == 0 else c - 1
+        pltpu.make_async_remote_copy(
+            src_ref=tiles.at[source, q], dst_ref=tiles.at[source, q],
+            send_sem=zs.at[way, d, q], recv_sem=zr.at[way, d, q],
+            device_id={"col": peer}, device_id_type=MESH).wait_recv()
+
+    side_x, side_y, side_c = at(0, 1, 0), at(1, 0, 0), at(0, 0, 1)
+    diag = at(1, 1, 0)
+
+    def region(u, who, part):
+        if part is None:
+            return right.at[u, pl.ds(who * rows_b, rows_b)]
+        return right.at[u, pl.ds(who * rows_b + part * half, half)]
+
+    def sent(u, k):
+        src, dst, to = [
+            (region(u, r, None), region(u, r, None), side_x),
+            (region(u, r, None), region(u, r, None), side_y),
+            (region(u, r, None), region(u, r, None), side_c),
+            (region(u, side_x, 0), region(u, side_x, 0), side_y),
+            (region(u, side_y, 1), region(u, side_y, 1), side_x),
+            (region(u, side_x, None), region(u, side_x, None), side_c),
+            (region(u, side_y, None), region(u, side_y, None), side_c),
+            (region(u, diag, 0), region(u, diag, 0), side_c),
+            (region(u, diag, 1), region(u, diag, 1), side_c),
+        ][k]
+        return pltpu.make_async_remote_copy(
+            src_ref=src, dst_ref=dst, send_sem=xs.at[u, k], recv_sem=xr.at[u, k],
+            device_id={"row": to}, device_id_type=MESH)
+
+    def landed(u, k):
+        where, to = [
+            (region(u, side_x, None), side_x),
+            (region(u, side_y, None), side_y),
+            (region(u, side_c, None), side_c),
+            (region(u, diag, 0), side_y),
+            (region(u, diag, 1), side_x),
+            (region(u, at(0, 1, 1), None), side_c),
+            (region(u, at(1, 0, 1), None), side_c),
+            (region(u, at(1, 1, 1), 0), side_c),
+            (region(u, at(1, 1, 1), 1), side_c),
+        ][k]
+        pltpu.make_async_remote_copy(
+            src_ref=where, dst_ref=where, send_sem=xs.at[u, k], recv_sem=xr.at[u, k],
+            device_id={"row": to}, device_id_type=MESH).wait_recv()
+
+    def begin(u):
+        right[u, pl.ds(r * rows_b, rows_b)] = tiles[u, c].reshape(rows_b, blk, wide)
+        for k in range(3):
+            sent(u, k).start()
+
+    def second(u):
+        landed(u, 0)
+        sent(u, 3).start()
+        sent(u, 5).start()
+        landed(u, 1)
+        sent(u, 4).start()
+        sent(u, 6).start()
+
+    def third(u):
+        landed(u, 3)
+        sent(u, 7).start()
+        landed(u, 4)
+        sent(u, 8).start()
+
+    for i in range(n):
+        @pl.when(c > 0)
+        def _():
+            zcopy(0, 0, i, c).start()
+
+        @pl.when(c < n - 1)
+        def _():
+            zcopy(1, 0, n - 1 - i, c).start()
+        if i == 0:
+            begin(c)
+
+    def begun_at(stage, act):
+        if stage == -1:
+            act(c)
+        for d in range(1, n):
+            @pl.when((c == stage) & (c + d < n))
+            def _():
+                act(c + d)
+
+            @pl.when((n - 1 - c == stage) & (c - d >= 0))
+            def _():
+                act(c - d)
+
+    for i in range(n + 1):
+        if i < n:
+            for d in range(1, n):
+                @pl.when(c + d < n)
+                def _():
+                    zarrive(0, d - 1, i, c + d)
+
+                    @pl.when(c > 0)
+                    def _():
+                        if d < n - 1:
+                            zcopy(0, d, i, c + d).start()
+
+                    @pl.when(c == i)
+                    def _():
+                        begin(c + d)
+
+                @pl.when(c - d >= 0)
+                def _():
+                    zarrive(1, d - 1, n - 1 - i, c - d)
+
+                    @pl.when(c < n - 1)
+                    def _():
+                        if d < n - 1:
+                            zcopy(1, d, n - 1 - i, c - d).start()
+
+                    @pl.when(c == n - 1 - i)
+                    def _():
+                        begin(c - d)
+        begun_at(i - 1, second)
+        begun_at(i - 2, third)
+    begun_at(n - 1, third)
+
+    for u in range(n):
+        for k in (2, 5, 6, 7, 8):
+            landed(u, k)
+
+    for z in range(n):
+        def product(u, carry):
+            for p in range(cols_b):
+                rhs[pl.ds(p * blk, blk), :] = right[u, tab[z * cols_b + p]]
+            lhs = jnp.concatenate([tiles[z, q] for q in range(n)], axis=1)
+            part = jnp.dot(lhs, rhs[...], preferred_element_type=jnp.float32)
+            for k in range(each):
+                cut = part[:, k * blk:(k + 1) * blk]
+                if z == 0:
+                    work[u * each + k] = cut
+                else:
+                    work[u * each + k] += cut
+            return carry
+        lax.fori_loop(0, n, product, 0)
+
+    for s in range(cols_b):
+        p = tab[nblk + s]
+        acc = jnp.zeros((1, blk), jnp.float32)
+        for i in range(rows_b):
+            keep = tab[masks + rows_b * cols_b + i * cols_b + s].astype(jnp.float32)
+            x = work[p, pl.ds(i * blk, blk), :]
+            x = x * x * keep
+            out[pl.ds(i * blk, blk), pl.ds(s * blk, blk)] = x
+            acc = acc + jnp.sum(x, axis=0, keepdims=True)
+        sums_b[0, :, pl.ds(s * blk, blk)] = acc
+    colsum = total_over_row(sums_b, bs, br)
+    out[...] = (jnp.float32(nodes) * out[...]) / colsum
+
+    for i in range(n):
+        for d in range(n - 1):
+            @pl.when((c > 0) & (c + d < n))
+            def _():
+                zcopy(0, d, i, c + d).wait_send()
+
+            @pl.when((c < n - 1) & (c - d >= 0))
+            def _():
+                zcopy(1, d, i, c - d).wait_send()
+    for u in range(n):
+        for k in range(9):
+            sent(u, k).wait_send()
+
+
+def fused(values, pattern, pruning, owners):
+    rows, cols = values.shape
+    n = lax.axis_size("col")
+    nodes = n * cols
+    tab = tables(pattern, pruning, owners, rows // BLK, cols // BLK, n)
+    dma = pltpu.SemaphoreType.DMA
+    return pl.pallas_call(
+        functools.partial(kernel, n, nodes),
+        out_shape=jax.ShapeDtypeStruct((rows, cols), jnp.float32),
+        in_specs=[pl.BlockSpec(memory_space=pltpu.SMEM), pl.BlockSpec(memory_space=pl.ANY)],
+        out_specs=pl.BlockSpec(memory_space=pltpu.VMEM),
+        scratch_shapes=[
+            pltpu.VMEM((n, n, rows, cols // n), jnp.bfloat16),
+            pltpu.VMEM((n, nodes // BLK, BLK, cols // n), jnp.bfloat16),
+            pltpu.VMEM((cols // BLK, rows, BLK), jnp.float32),
+            pltpu.VMEM((cols // BLK, rows, BLK), jnp.float32),
+            pltpu.VMEM((8, 1, cols), jnp.float32),
+            pltpu.VMEM((8, 1, cols), jnp.float32),
+            pltpu.VMEM((cols, cols // n), jnp.bfloat16),
+            dma((cols // BLK,)),
+            dma((2, n - 1, n)),
+            dma((2, n - 1, n)),
+            dma((n, 9)),
+            dma((n, 9)),
+            dma((7,)),
+            dma((7,)),
+            dma((7,)),
+            dma((7,)),
+        ],
+        compiler_params=pltpu.CompilerParams(
+            collective_id=0, has_side_effects=True, vmem_limit_bytes=44 * 2**20
+        ),
+        cost_estimate=pl.CostEstimate(
+            flops=2 * rows * nodes * cols, bytes_accessed=8 * rows * cols, transcendentals=0
+        ),
+    )(tab, values)
+
+
 def solution(mesh):
+    nrows, ncols = mesh.shape["row"], mesh.shape["col"]
+
+    def program(values, pattern, pruning, owners):
+        rows, cols = values.shape
+        packed = nrows == 8 and owners.shape[0] == 2 * ncols * ncols
+        return (fused if packed else body)(values, pattern, pruning, owners)
+
     return jax.shard_map(
-        body,
+        program,
         mesh=mesh,
         in_specs=(P("row", "col"), P(), P(), P()),
         out_specs=P("row", "col"),

time: 213 us -> 98.7 us (0.46)
  waiting for transfers between devices: 143 us -> 0 us
  Pallas kernels: 0 us -> 92.3 us
  blocking collectives: 28.2 us -> 0 us
  between operations: 13.5 us -> 0.02 us
  matrix products: 10.5 us -> 0 us
  starting transfers between devices: 4.87 us -> 0 us
  other arithmetic: 7.02 us -> 2.27 us
    pallas_call x0 -> x1, Pallas kernels: none -> 92.3 us  [fused(): pl.pallas_call(functools.partial(kernel, n, nodes), out_shape=jax.ShapeDt...]
    all_gather x2 -> x0, waiting for transfers between devices: 91.7 us -> none  [the longest x1 54.9 us: body(): lax.all_gather(right_operand, 'row', axis=0, tiled=True)]
    all_to_all x1 -> x0, waiting for transfers between devices: 51.6 us -> none  [body(): lax.all_to_all(pack_blocks(stochastic, owners, me_col, ncols, capacity, b...]
    psum x2 -> x0, blocking collectives: 28.2 us -> none  [the longest x1 15.1 us: body(): colsum_in = lax.psum(jnp.sum(masked, axis=0), 'row')]
    dot_general x4 -> x0, matrix products: 10.5 us -> none  [the longest x1 8.44 us: body(): jnp.dot(row_panel, lax.all_gather(right_operand, 'row', axis=0, tiled=Tru...]
    all_to_all x1 -> x0, starting transfers between devices: 4.87 us -> none  [body(): lax.all_to_all(pack_blocks(stochastic, owners, me_col, ncols, capacity, b...]
    convert_element_type x3 -> x0, other arithmetic: 4.13 us -> none  [the longest x1 3.21 us: body(): stochastic = (masked / colsum_in[None, :]).astype(jnp.bfloat16)]
  transfers between devices with their start and end apart: 3 -> 0, of which waited for: 3 -> 0; matrix products, arithmetic and copies ran while one was open for 3% -> 0% of each run, Pallas kernels for 0% -> 0%
where the time goes in v1:
time: 98.7 us; the launch traced here: 98.5 us
  Pallas kernels  92.3 us (94%)
  local copies, waits for them, and re-layouts  3.89 us (4%)
  other arithmetic  2.27 us (2%)
    pallas_call x1, Pallas kernels, fused(): pl.pallas_call(functools.partial(kernel, n, nodes), out_shape=jax.ShapeDt...  92.3 us
    unnamed x3, local copies, waits for them, and re-layouts  2.92 us

profile of v1, /device:TPU:0, one launch (start us, length us, event | category | flops | bytes accessed | tf_op | source)
XLA Modules:
  0.0 98.5 jit_solution(469187507949848263)
XLA Ops:
  0.0 0.7 and_select_fusion
  0.7 0.1 select_reduce_fusion.3
  0.8 0.9 fusion.2
  1.6 0.1 select_reduce_fusion.2
  1.8 0.1 broadcast_subtract_fusion
  1.8 0.1 iota_compare_fusion.2
  1.9 0.1 iota_compare_fusion.3
  2.0 0.7 constant_dynamic-slice_fusion
  2.7 0.1 select_reduce_fusion.1
  2.8 0.1 reshape.92
  2.9 0.2 select_reduce_fusion
  3.1 0.1 reshape.93
  3.2 0.1 concatenate.3.tab
  3.2 0.0 copy-start
  3.2 1.6 %copy-done = f32[512,1024]{1,0:T(8,128)S(1)} copy-done((f32[512,1024]{1,0:T(8,128)S(1)}, f32[512,1024]{1,0:T(8,128)}, u32[]{:S(2)}) %copy-start) | copy-done | bytes 2097176
  4.9 92.3 %shard_map.46 = f32[512,1024]{1,0:T(8,128)S(1)} custom-call(s32[112]{0:T(128)S(1)} %concatenate.3.tab, f32[512,1024]{1,0:T(8,128)S(1)} %copy-done), custom_call_target="tpu_custom_call" | custom-call | flops 4294967296 | bytes 4194304 | tf_op jit(solution)/shard_map/pallas_call | solution.py:394
  97.2 1.3 %copy.6 = f32[512,1024]{1,0:T(8,128)} copy(f32[512,1024]{1,0:T(8,128)S(1)} %shard_map.46) | data formatting | bytes 4194304
  (2 shorter events, 0.0 us)
Async XLA Ops:
  3.2 1.6 %copy-start = (f32[512,1024]{1,0:T(8,128)S(1)}, f32[512,1024]{1,0:T(8,128)}, u32[]{:S(2)}) copy-start(f32[512,1024]{1,0:T(8,128)} %values.1) | copy-start | bytes 6291460

commit v2 on v1

--- a/solution.py
+++ b/solution.py
@@ -110,34 +110,8 @@
 MESH = pl.DeviceIdType.MESH
 
 
-def tables(pattern, pruning, owners, rows_b, cols_b, ncols):
-    me_row = lax.axis_index("row")
-    me_col = lax.axis_index("col")
-    nblk = owners.shape[0]
-    ids = jnp.arange(nblk)
-    source = ids // cols_b
-    dest = owners // cols_b
-    same = (source[:, None] == source[None, :]) & (dest[:, None] == dest[None, :])
-    rank = jnp.sum(jnp.where(same & (ids[:, None] < ids[None, :]), 1, 0), axis=0)
-    cap = cols_b // ncols
-    packed = source * cols_b + dest * cap + rank
-    order = jnp.sum(jnp.where(packed[None, :] == ids[:, None], ids[None, :], 0), axis=1)
-    wanted = me_col * cols_b + jnp.arange(cols_b)
-    hit = owners[None, :] == wanted[:, None]
-    pos = jnp.sum(jnp.where(hit, (source * cap + rank)[None, :], 0), axis=1)
-    from_block = jnp.sum(jnp.where(hit, ids[None, :], 0), axis=1)
-    mine = lax.dynamic_slice(order, (me_col * cols_b,), (cols_b,))
-    prow = lax.dynamic_slice(pattern, (me_row * rows_b, 0), (rows_b, nblk))
-    prow = jnp.sum(jnp.where(mine[None, :, None] == ids[None, None, :], prow[:, None, :], 0), axis=2)
-    krow = lax.dynamic_slice(pruning, (me_row * rows_b, 0), (rows_b, nblk))
-    kept = jnp.sum(jnp.where(from_block[None, :, None] == ids[None, None, :], krow[:, None, :], 0), axis=2)
-    return jnp.concatenate(
-        [order, pos, prow.reshape(-1), kept.reshape(-1), mine - me_col * cols_b]
-    ).astype(jnp.int32)
-
-
-def kernel(n, nodes, tab, values, out, tiles, right, scores, work, sums_a, sums_b, rhs,
-           load_sem, zs, zr, xs, xr, as_, ar, bs, br):
+def kernel(n, nodes, own, pattern, pruning, values, out, tiles, right, scores, work, left, late,
+           sums_a, sums_b, invs, rhs, tab, load_sem, zs, zr, xs, xr, as_, ar, bs, br, cs, cr):
     rows, cols = values.shape
     blk = BLK
     rows_b, cols_b = rows // blk, cols // blk
@@ -166,50 +140,35 @@
     barrier = pltpu.get_barrier_semaphore()
     for peer in others:
         pl.semaphore_signal(barrier, inc=1, device_id={"row": peer}, device_id_type=MESH)
-
-    @pl.when(c > 0)
-    def _():
-        pl.semaphore_signal(barrier, inc=1, device_id={"col": c - 1}, device_id_type=MESH)
-
-    @pl.when(c < n - 1)
-    def _():
-        pl.semaphore_signal(barrier, inc=1, device_id={"col": c + 1}, device_id_type=MESH)
-
-    def total_over_row(sums, ssem, rsem):
-        for f, peer in enumerate(others):
+    for d in range(1, n):
+        pl.semaphore_signal(barrier, inc=1, device_id={"col": (c + d) % n}, device_id_type=MESH)
+
+    def chosen(keys, key, options):
+        found = options[0]
+        for k, option in zip(keys[1:], options[1:]):
+            found = jnp.where(k == key, option, found)
+        return found
+
+    def order_of(base):
+        dest = [lax.div(own[base + k], cols_b) for k in range(cols_b)]
+        place = []
+        for k in range(cols_b):
+            rank = sum([jnp.where(dest[i] == dest[k], 1, 0) for i in range(k)], 0)
+            place.append(dest[k] * each + rank)
+        return [chosen(place, p, range(cols_b)) for p in range(cols_b)]
+
+    def row_copies(sums, ssem, rsem):
+        return [
             pltpu.make_async_remote_copy(
                 src_ref=sums.at[0], dst_ref=sums.at[f + 1], send_sem=ssem.at[f], recv_sem=rsem.at[f],
-                device_id={"row": peer}, device_id_type=MESH).start()
-        for f, peer in enumerate(others):
-            pltpu.make_async_remote_copy(
-                src_ref=sums.at[0], dst_ref=sums.at[f + 1], send_sem=ssem.at[f], recv_sem=rsem.at[f],
-                device_id={"row": peer}, device_id_type=MESH).wait()
+                device_id={"row": peer}, device_id_type=MESH)
+            for f, peer in enumerate(others)
+        ]
+
+    def total_of(sums):
         terms = [sums[f] for f in range(8)]
         pair = [terms[i] + terms[i + 1] for i in range(0, 8, 2)]
-        quad = [pair[0] + pair[1], pair[2] + pair[3]]
-        return quad[0] + quad[1]
-
-    for load in loads:
-        load.wait()
-    masks = nblk + cols_b
-    local = masks + 2 * rows_b * cols_b
-    for p in range(cols_b):
-        b = tab[local + p]
-        acc = jnp.zeros((1, blk), jnp.float32)
-        for i in range(rows_b):
-            keep = tab[masks + i * cols_b + p].astype(jnp.float32)
-            x = scores[b, pl.ds(i * blk, blk), :] * keep
-            work[p, pl.ds(i * blk, blk), :] = x
-            acc = acc + jnp.sum(x, axis=0, keepdims=True)
-        sums_a[0, :, pl.ds(p * blk, blk)] = acc
-
-    ends = jnp.where(c == 0, 1, 0) + jnp.where(c == n - 1, 1, 0)
-    pl.semaphore_wait(barrier, 9 - ends)
-
-    colsum = total_over_row(sums_a, as_, ar)
-    for p in range(cols_b):
-        part = work[p] / colsum[:, p * blk:(p + 1) * blk]
-        tiles[c, p // each, :, pl.ds(p % each * blk, blk)] = part.astype(jnp.bfloat16)
+        return (pair[0] + pair[1]) + (pair[2] + pair[3])
 
     def zcopy(way, d, q, source):
         target = c - 1 if way == 0 else c + 1
@@ -284,16 +243,108 @@
         landed(u, 4)
         sent(u, 8).start()
 
-    for i in range(n):
+    mine = order_of(c * cols_b)
+    for load in loads:
+        load.wait()
+    pl.semaphore_wait(barrier, 7 + n - 1)
+    made = []
+    for i in range((n + 1) // 2):
+        made += [i, n - 1 - i] if i != n - 1 - i else [i]
+    for q in made:
+        for k in range(each):
+            b = mine[q * each + k]
+            acc = jnp.zeros((1, blk), jnp.float32)
+            for i in range(rows_b):
+                keep = pattern[r * rows_b + i, c * cols_b + b].astype(jnp.float32)
+                x = scores[b, pl.ds(i * blk, blk), :] * keep
+                tiles[c, q, pl.ds(i * blk, blk), pl.ds(k * blk, blk)] = x.astype(jnp.bfloat16)
+                acc = acc + jnp.sum(x, axis=0, keepdims=True)
+            sums_a[0, q, :, pl.ds(k * blk, blk)] = acc
+
         @pl.when(c > 0)
         def _():
-            zcopy(0, 0, i, c).start()
+            zcopy(0, 0, q, c).start()
 
         @pl.when(c < n - 1)
         def _():
-            zcopy(1, 0, n - 1 - i, c).start()
-        if i == 0:
-            begin(c)
+            zcopy(1, 0, q, c).start()
+    for copy in row_copies(sums_a, as_, ar):
+        copy.start()
+    begin(c)
+
+    for z in range(n):
+        for p, b in enumerate(order_of(z * cols_b)):
+            tab[z * cols_b + p] = z * cols_b + b
+    came = [tab[u * cols_b + c * each + k] for u in range(n) for k in range(each)]
+    goes = [own[b] - c * cols_b for b in came]
+
+    for copy in row_copies(sums_a, as_, ar):
+        copy.wait()
+    invs[c] = 1.0 / total_of(sums_a)
+
+    def scales(d):
+        return pltpu.make_async_remote_copy(
+            src_ref=invs.at[c], dst_ref=invs.at[c], send_sem=cs.at[d - 1], recv_sem=cr.at[d - 1],
+            device_id={"col": (c + d) % n}, device_id_type=MESH)
+
+    for d in range(1, n):
+        scales(d).start()
+
+    def scales_landed():
+        for d in range(1, n):
+            source = (c + n - d) % n
+            pltpu.make_async_remote_copy(
+                src_ref=invs.at[source], dst_ref=invs.at[source],
+                send_sem=cs.at[d - 1], recv_sem=cr.at[d - 1],
+                device_id={"col": source}, device_id_type=MESH).wait_recv()
+
+    last = jnp.where(c < n // 2, n - 1, 0)
+
+    def scaled(z, q):
+        return (tiles[z, q].astype(jnp.float32) * invs[z, q]).astype(jnp.bfloat16)
+
+    def early_product():
+        scales_landed()
+        for u in range(n):
+            for k in (2, 5, 6, 7, 8):
+                landed(u, k)
+        for z in range(n):
+            for j in range(n - 1):
+                left[:, pl.ds(j * wide, wide)] = scaled(z, (last + 1 + j) % n)
+
+            def product(u, carry):
+                for j in range(n - 1):
+                    q = (last + 1 + j) % n
+                    for k in range(each):
+                        rhs[pl.ds((j * each + k) * blk, blk), :] = right[u, tab[z * cols_b + q * each + k]]
+                part = jnp.dot(
+                    left[...], rhs[pl.ds(0, (n - 1) * wide), :], preferred_element_type=jnp.float32)
+                for k in range(each):
+                    cut = part[:, k * blk:(k + 1) * blk]
+                    if z == 0:
+                        work[u * each + k] = cut
+                    else:
+                        work[u * each + k] += cut
+                return carry
+            lax.fori_loop(0, n, product, 0)
+
+    def late_product():
+        for z in range(n):
+            late[:, pl.ds(z * wide, wide)] = scaled(z, last)
+
+        def product(u, carry):
+            for z in range(n):
+                for k in range(each):
+                    rhs[pl.ds((z * each + k) * blk, blk), :] = right[u, tab[z * cols_b + last * each + k]]
+            part = jnp.dot(late[...], rhs[...], preferred_element_type=jnp.float32)
+            scale = invs[u, c]
+            for k in range(each):
+                piece = slice(k * blk, (k + 1) * blk)
+                work[u * each + k] = (work[u * each + k] + part[:, piece]) * scale[:, piece]
+            return carry
+        lax.fori_loop(0, n, product, 0)
+
+    at_end = (c == 0) | (c == n - 1)
 
     def begun_at(stage, act):
         if stage == -1:
@@ -308,6 +359,10 @@
                 act(c - d)
 
     for i in range(n + 1):
+        if i == n - 1:
+            @pl.when(at_end)
+            def _():
+                early_product()
         if i < n:
             for d in range(1, n):
                 @pl.when(c + d < n)
@@ -339,38 +394,32 @@
         begun_at(i - 2, third)
     begun_at(n - 1, third)
 
-    for u in range(n):
-        for k in (2, 5, 6, 7, 8):
-            landed(u, k)
-
-    for z in range(n):
-        def product(u, carry):
-            for p in range(cols_b):
-                rhs[pl.ds(p * blk, blk), :] = right[u, tab[z * cols_b + p]]
-            lhs = jnp.concatenate([tiles[z, q] for q in range(n)], axis=1)
-            part = jnp.dot(lhs, rhs[...], preferred_element_type=jnp.float32)
-            for k in range(each):
-                cut = part[:, k * blk:(k + 1) * blk]
-                if z == 0:
-                    work[u * each + k] = cut
-                else:
-                    work[u * each + k] += cut
-            return carry
-        lax.fori_loop(0, n, product, 0)
+    @pl.when(jnp.logical_not(at_end))
+    def _():
+        early_product()
+
+    late_product()
 
     for s in range(cols_b):
-        p = tab[nblk + s]
+        p = chosen(goes, s, range(cols_b))
+        b = chosen(goes, s, came)
         acc = jnp.zeros((1, blk), jnp.float32)
         for i in range(rows_b):
-            keep = tab[masks + rows_b * cols_b + i * cols_b + s].astype(jnp.float32)
+            keep = pruning[r * rows_b + i, b].astype(jnp.float32)
             x = work[p, pl.ds(i * blk, blk), :]
             x = x * x * keep
             out[pl.ds(i * blk, blk), pl.ds(s * blk, blk)] = x
             acc = acc + jnp.sum(x, axis=0, keepdims=True)
         sums_b[0, :, pl.ds(s * blk, blk)] = acc
-    colsum = total_over_row(sums_b, bs, br)
-    out[...] = (jnp.float32(nodes) * out[...]) / colsum
-
+    for copy in row_copies(sums_b, bs, br):
+        copy.start()
+    for copy in row_copies(sums_b, bs, br):
+        copy.wait()
+    inv_out = 1.0 / total_of(sums_b)
+    out[...] = (out[...] * inv_out) * jnp.float32(nodes)
+
+    for d in range(1, n):
+        scales(d).wait_send()
     for i in range(n):
         for d in range(n - 1):
             @pl.when((c > 0) & (c + d < n))
@@ -389,21 +438,24 @@
     rows, cols = values.shape
     n = lax.axis_size("col")
     nodes = n * cols
-    tab = tables(pattern, pruning, owners, rows // BLK, cols // BLK, n)
     dma = pltpu.SemaphoreType.DMA
     return pl.pallas_call(
         functools.partial(kernel, n, nodes),
         out_shape=jax.ShapeDtypeStruct((rows, cols), jnp.float32),
-        in_specs=[pl.BlockSpec(memory_space=pltpu.SMEM), pl.BlockSpec(memory_space=pl.ANY)],
+        in_specs=[pl.BlockSpec(memory_space=pltpu.SMEM)] * 3 + [pl.BlockSpec(memory_space=pl.ANY)],
         out_specs=pl.BlockSpec(memory_space=pltpu.VMEM),
         scratch_shapes=[
             pltpu.VMEM((n, n, rows, cols // n), jnp.bfloat16),
             pltpu.VMEM((n, nodes // BLK, BLK, cols // n), jnp.bfloat16),
             pltpu.VMEM((cols // BLK, rows, BLK), jnp.float32),
             pltpu.VMEM((cols // BLK, rows, BLK), jnp.float32),
+            pltpu.VMEM((rows, cols - cols // n), jnp.bfloat16),
+            pltpu.VMEM((rows, cols), jnp.bfloat16),
+            pltpu.VMEM((8, n, 1, cols // n), jnp.float32),
             pltpu.VMEM((8, 1, cols), jnp.float32),
-            pltpu.VMEM((8, 1, cols), jnp.float32),
+            pltpu.VMEM((n, n, 1, cols // n), jnp.float32),
             pltpu.VMEM((cols, cols // n), jnp.bfloat16),
+            pltpu.SMEM((nodes // BLK,), jnp.int32),
             dma((cols // BLK,)),
             dma((2, n - 1, n)),
             dma((2, n - 1, n)),
@@ -413,6 +465,8 @@
             dma((7,)),
             dma((7,)),
             dma((7,)),
+            dma((n - 1,)),
+            dma((n - 1,)),
         ],
         compiler_params=pltpu.CompilerParams(
             collective_id=0, has_side_effects=True, vmem_limit_bytes=44 * 2**20
@@ -420,7 +474,7 @@
         cost_estimate=pl.CostEstimate(
             flops=2 * rows * nodes * cols, bytes_accessed=8 * rows * cols, transcendentals=0
         ),
-    )(tab, values)
+    )(owners, pattern, pruning, values)
 
 
 def solution(mesh):

time: 98.7 us -> 89.2 us (0.904)
  Pallas kernels: 92.3 us -> 83.8 us
  other arithmetic: 2.27 us -> 0 us
  local copies, waits for them, and re-layouts: 3.89 us -> 5 us
    pallas_call x1, Pallas kernels: 92.3 us -> 83.8 us  [fused(): pl.pallas_call(functools.partial(kernel, n, nodes), out_shape=jax.ShapeDt...]
    unnamed x3 -> x9, local copies, waits for them, and re-layouts: 2.92 us -> 5 us
    reduce_sum x5 -> x0, other arithmetic: 1.37 us -> none  [the longest x1 0.86 us: tables(): from_block = jnp.sum(jnp.where(hit, ids[None, :], 0), axis=1)]
where the time goes in v2:
time: 89.2 us; the launch traced here: 88.8 us
  Pallas kernels  83.8 us (94%)
  local copies, waits for them, and re-layouts  5 us (6%)
    pallas_call x1, Pallas kernels, fused(): pl.pallas_call(functools.partial(kernel, n, nodes), out_shape=jax.ShapeDt...  83.8 us
    unnamed x9, local copies, waits for them, and re-layouts  5 us

profile of v2, /device:TPU:0, one launch (start us, length us, event | category | flops | bytes accessed | tf_op | source)
XLA Modules:
  0.0 88.8 jit_solution(4067270343818518406)
XLA Ops:
  0.0 0.0 copy-start
  0.0 1.6 %copy-done = f32[512,1024]{1,0:T(8,128)S(1)} copy-done((f32[512,1024]{1,0:T(8,128)S(1)}, f32[512,1024]{1,0:T(8,128)}, u32[]{:S(2)}) %copy-start) | copy-done | bytes 2097176
  1.6 0.0 copy-start.1
  1.6 0.7 copy-done.1
  2.3 0.0 copy-start.2
  2.3 0.7 copy-done.2
  3.0 0.0 copy-start.3
  3.0 0.7 copy-done.3
  3.7 83.8 %shard_map.46 = f32[512,1024]{1,0:T(8,128)S(1)} custom-call(s32[32]{0:T(128)S(1)} %copy-done.3, s32[32,32]{1,0:T(8,128)S(1)} %copy-done.1, s32[32,32]{1,0:T(8,128)S(1)} %copy-done.2, f32[512,1024]{1,0:T(8,128)S(1)} %copy-done), custom_call_target="tpu_custom_call" | custom-call | flops 4294967296 | bytes 4194304 | tf_op jit(solution)/shard_map/pallas_call | solution.py:442
  87.5 1.3 %copy.6 = f32[512,1024]{1,0:T(8,128)} copy(f32[512,1024]{1,0:T(8,128)S(1)} %shard_map.46) | data formatting | bytes 4194304
Async XLA Ops:
  0.0 1.6 %copy-start = (f32[512,1024]{1,0:T(8,128)S(1)}, f32[512,1024]{1,0:T(8,128)}, u32[]{:S(2)}) copy-start(f32[512,1024]{1,0:T(8,128)} %values.1) | copy-start | bytes 6291460
  1.6 0.7 copy-start.1
  2.3 0.7 copy-start.2
  3.0 0.7 copy-start.3

commit v3 on v2

--- a/solution.py
+++ b/solution.py
@@ -469,7 +469,7 @@
             dma((n - 1,)),
         ],
         compiler_params=pltpu.CompilerParams(
-            collective_id=0, has_side_effects=True, vmem_limit_bytes=44 * 2**20
+            collective_id=0, has_side_effects=True, vmem_limit_bytes=62 * 2**20
         ),
         cost_estimate=pl.CostEstimate(
             flops=2 * rows * nodes * cols, bytes_accessed=8 * rows * cols, transcendentals=0

time: 89.2 us -> 88.7 us (level)
  local copies, waits for them, and re-layouts: 5 us -> 3.16 us
  Pallas kernels: 83.8 us -> 85.2 us
    unnamed x9 -> x1, local copies, waits for them, and re-layouts: 5 us -> 3.16 us
    pallas_call x1, Pallas kernels: 83.8 us -> 85.2 us  [fused(): pl.pallas_call(functools.partial(kernel, n, nodes), out_shape=jax.ShapeDt...]
where the time goes in v3:
time: 88.7 us; the launch traced here: 88.4 us
  Pallas kernels  85.2 us (96%)
  local copies, waits for them, and re-layouts  3.16 us (4%)
    pallas_call x1, Pallas kernels, fused(): pl.pallas_call(functools.partial(kernel, n, nodes), out_shape=jax.ShapeDt...  85.2 us
    unnamed x1, local copies, waits for them, and re-layouts  3.16 us

profile of v3, /device:TPU:0, one launch (start us, length us, event | category | flops | bytes accessed | tf_op | source)
XLA Modules:
  0.0 88.4 jit_solution(3976607737193213444)
XLA Ops:
  0.0 85.2 %shard_map.46 = f32[512,1024]{1,0:T(8,128)} custom-call(s32[32]{0:T(128)} %own.1, s32[32,32]{1,0:T(8,128)} %pattern.1, s32[32,32]{1,0:T(8,128)} %pruning.1, f32[512,1024]{1,0:T(8,128)} %values.1), custom_call_target="tpu_custom_call" | custom-call | flops 4294967296 | bytes 4194304 | tf_op jit(solution)/shard_map/pallas_call | solution.py:442
  85.3 3.2 %copy.6 = f32[512,1024]{1,0:T(8,128)} copy(f32[512,1024]{1,0:T(8,128)} %shard_map.46) | data formatting | bytes 4194304

commit v4 on v3

--- a/solution.py
+++ b/solution.py
@@ -416,7 +416,7 @@
     for copy in row_copies(sums_b, bs, br):
         copy.wait()
     inv_out = 1.0 / total_of(sums_b)
-    out[...] = (out[...] * inv_out) * jnp.float32(nodes)
+    out[...] = out[...] * inv_out
 
     for d in range(1, n):
         scales(d).wait_send()
@@ -439,7 +439,7 @@
     n = lax.axis_size("col")
     nodes = n * cols
     dma = pltpu.SemaphoreType.DMA
-    return pl.pallas_call(
+    shares = pl.pallas_call(
         functools.partial(kernel, n, nodes),
         out_shape=jax.ShapeDtypeStruct((rows, cols), jnp.float32),
         in_specs=[pl.BlockSpec(memory_space=pltpu.SMEM)] * 3 + [pl.BlockSpec(memory_space=pl.ANY)],
@@ -475,6 +475,7 @@
             flops=2 * rows * nodes * cols, bytes_accessed=8 * rows * cols, transcendentals=0
         ),
     )(owners, pattern, pruning, values)
+    return jnp.float32(nodes) * shares
 
 
 def solution(mesh):

time: 88.7 us -> 88.7 us (level)
  other arithmetic: 0 us -> 3.22 us
  local copies, waits for them, and re-layouts: 3.16 us -> 0 us
    mul x0 -> x1, other arithmetic: none -> 3.22 us  [fused(): return jnp.float32(nodes) * shares]
    unnamed x1 -> x0, local copies, waits for them, and re-layouts: 3.16 us -> none
where the time goes in v4:
time: 88.7 us; the launch traced here: 88.5 us
  Pallas kernels  85.2 us (96%)
  other arithmetic  3.22 us (4%)
    pallas_call x1, Pallas kernels, fused(): pl.pallas_call(functools.partial(kernel, n, nodes), out_shape=jax.ShapeDt...  85.2 us
    mul x1, other arithmetic, fused(): return jnp.float32(nodes) * shares  3.22 us

profile of v4, /device:TPU:0, one launch (start us, length us, event | category | flops | bytes accessed | tf_op | source)
XLA Modules:
  0.0 88.5 jit_solution(17046465266626093413)
XLA Ops:
  0.0 85.2 %shard_map.46 = f32[512,1024]{1,0:T(8,128)} custom-call(s32[32]{0:T(128)} %own.1, s32[32,32]{1,0:T(8,128)} %pattern.1, s32[32,32]{1,0:T(8,128)} %pruning.1, f32[512,1024]{1,0:T(8,128)} %values.1), custom_call_target="tpu_custom_call" | custom-call | flops 4294967296 | bytes 4194304 | tf_op jit(solution)/shard_map/pallas_call | solution.py:442
  85.3 3.2 %broadcast_multiply_fusion = f32[512,1024]{1,0:T(8,128)} fusion(f32[512,1024]{1,0:T(8,128)} %shard_map.46), kind=kLoop, calls=%fused_computation | loop fusion | flops 524288 | bytes 4194304 | tf_op jit(solution)/shard_map/mul | solution.py:478
